TPU v7x, 128 devices: a whole 4x4x4 slice. The times are simulated.
128 devices in a mesh: gx: 8 (over x, z_hi), gy: 4 (over y), gz: 4 (over z_lo, core).
Axes of the slice: x: 4, y: 4, z: 4 (z_hi: 2, z_lo: 2; z = z_hi * 2 + z_lo), core: 2. Of those that a mesh axis runs over, the one named last changes fastest.
Arguments:
- pre_act: bfloat16 [2048, 24576], P('gx', ('gy', 'gz')), may hold values from -6 to 6
- grad_out: bfloat16 [2048, 6144], P(('gx', 'gy'), 'gz'), may hold values from -0.3125 to 0.3125
- weight: bfloat16 [3072, 8, 6144], P('gy', 'gx', 'gz'), may hold values from -6 to 6
Outputs:
- pre_grad: bfloat16 [2048, 24576], P('gx', ('gy', 'gz'))
- weight_grad: bfloat16 [3072, 8, 6144], P('gy', 'gx', 'gz')
All inputs are finite; a program needn't handle non-finite values.
Results may differ from a plain program's by a relative error of at most 0.02.
Values may be sent and summed in bfloat16 or wider, within the bound.
No kernel may reach another device: no remote copies, remote signals or barrier semaphores. Data moves between devices by JAX's collectives and lax.ppermute only.
A program may use at most 128 MiB of HBM per device.

v0:
```python
import jax
import jax.numpy as jnp
from jax import lax
from jax.sharding import PartitionSpec as P

tanh_scale = 0.7978845608028654
cubic_coef = 0.044715


def gelu_parts(inputs):
    inner = tanh_scale * (inputs + cubic_coef * inputs * inputs * inputs)
    tangent = jnp.tanh(inner)
    gelu_value = 0.5 * inputs * (1.0 + tangent)
    gelu_slope = 0.5 * (1.0 + tangent) + 0.5 * inputs * (1.0 - tangent * tangent) * tanh_scale * (
        1.0 + 3.0 * cubic_coef * inputs * inputs
    )
    return (gelu_value, gelu_slope)


def per_device(pre_act, grad_out, weight):
    groups = lax.axis_size("gx")
    own_value, own_slope = gelu_parts(pre_act.astype(jnp.float32))
    full_pre = lax.all_gather(pre_act, "gz", axis=1, tiled=True)
    full_value, unused_slope = gelu_parts(full_pre.astype(jnp.float32))
    hidden = full_value.astype(jnp.bfloat16)
    token_count = hidden.shape[0]
    hidden_cols = hidden.shape[1]
    unit_rows = hidden_cols // groups
    hidden_split = hidden.reshape(token_count, unit_rows, groups).transpose(2, 0, 1)
    grad_rows = lax.all_gather(grad_out, "gy", axis=0, tiled=True)
    partial_block = jnp.einsum(
        "pd,rcd->cpr",
        grad_rows,
        lax.all_gather(weight, "gx", axis=1, tiled=True),
        preferred_element_type=jnp.float32,
    )
    reduced = lax.psum_scatter(
        jnp.einsum(
            "cpr,pd->crd", hidden_split, grad_rows, preferred_element_type=jnp.float32
        ).astype(jnp.bfloat16),
        "gx",
        scatter_dimension=0,
        tiled=True,
    ).astype(jnp.float32)
    weight_grad = reduced.transpose(1, 0, 2).astype(jnp.bfloat16)
    flat_partial = partial_block.transpose(1, 2, 0).reshape(token_count, hidden_cols)
    summed = lax.psum_scatter(
        flat_partial.astype(jnp.bfloat16), "gz", scatter_dimension=1, tiled=True
    ).astype(jnp.float32)
    pre_grad = (summed * own_slope).astype(jnp.bfloat16)
    return (pre_grad, weight_grad)


def solution(mesh):
    placed = (P("gx", ("gy", "gz")), P(("gx", "gy"), "gz"), P("gy", "gx", "gz"))
    return jax.shard_map(
        per_device,
        mesh=mesh,
        in_specs=placed,
        out_specs=(P("gx", ("gy", "gz")), P("gy", "gx", "gz")),
        check_vma=False,
    )
```

profile of v0, /device:TPU:0, one launch (start us, length us, event | category | flops | bytes accessed | tf_op | source)
XLA Modules:
  0.0 517.2 jit_solution(12451465716665459084)
XLA Ops:
  7.2 0.0 copy-start.1
  7.2 0.0 all-gather.3.cloned.1.call-start
  7.2 0.7 all-gather.3.cloned.1.call-update
  7.9 0.0 all-gather.5.cloned.1.call-start
  8.0 2.3 copy.12
  10.2 0.0 all-gather.5.cloned.1.call-update
  10.3 0.0 reduce-scatter.3.cloned.1.call-start
  10.3 0.0 copy-done.1
  10.3 13.9 %all_gather.9 = bf16[256,1536]{1,0:T(8,128)(2,1)S(1)} all-gather(bf16[64,1536]{1,0:T(8,128)(2,1)S(1)} %copy-done.1), channel_id=1, replica_groups=mesh['gx'=8,'gy'=4,'gz'=4] {'gy'}, dimensions={0}, use_global_device_ids=true | all-gather | bytes 983040 | tf_op jit(solution)/shard_map/all_gather | solution.py:30
  24.2 193.8 %all-gather.3.cloned.1.call-done = bf16[768,8,1536]{2,0,1:T(8,128)(2,1)} async-done(((bf16[768,1,1536]{2,0,1:T(8,128)(2,1)}), bf16[768,8,1536]{2,0,1:T(8,128)(2,1)}) %all-gather.3.cloned.1.call-update) | async-done | bytes 18874384 | tf_op jit(solution)/shard_map/all_gather | solution.py:34
  218.1 10.2 %convolution_convert_fusion.1 = bf16[256,768,8]{1,0,2:T(8,128)(2,1)} fusion(bf16[768,8,1536]{2,0,1:T(8,128)(2,1)} %all-gather.3.cloned.1.call-done, bf16[256,1536]{1,0:T(8,128)(2,1)S(1)} %all_gather.9), kind=kOutput, calls=%fused_computation.20 | convolution fusion | flops 4833411072 | bytes 22806528 | tf_op jit(solution)/shard_map/pd,rcd->cpr/dot_general | solution.py:31
  228.2 5.2 copy.11
  233.4 0.0 reduce-scatter.3.cloned.1.call-update
  233.4 0.0 reduce-scatter.5.cloned.1.call-start
  233.5 22.1 %all-gather.5.cloned.1.call-done = bf16[256,6144]{0,1:T(8,128)(2,1)} async-done(((bf16[256,1536]{0,1:T(8,128)(2,1)}), bf16[256,6144]{0,1:T(8,128)(2,1)}) %all-gather.5.cloned.1.call-update) | async-done | bytes 3145744 | tf_op jit(solution)/shard_map/all_gather | solution.py:23
  255.6 3.6 fusion.5
  259.2 9.5 %convolution_convert_fusion = bf16[8,768,1536]{2,1,0:T(8,128)(2,1)} fusion(bf16[8,256,768]{1,0,2:T(8,128)(2,1)S(1)} %fusion.5, bf16[256,1536]{1,0:T(8,128)(2,1)S(1)} %all_gather.9), kind=kOutput, calls=%fused_computation | convolution fusion | flops 4841275392 | bytes 22806528 | tf_op jit(solution)/shard_map/cpr,pd->crd/dot_general | solution.py:38
  268.6 0.0 copy-start
  268.6 0.0 reduce-scatter.5.cloned.1.call-update
  268.7 27.5 %reduce-scatter.3.cloned.1.call-done = bf16[256,1536]{0,1:T(8,128)(2,1)} async-done(((bf16[256,6144]{0,1:T(8,128)(2,1)}), bf16[256,1536]{0,1:T(8,128)(2,1)}) %reduce-scatter.3.cloned.1.call-update) | async-done | bytes 786448 | tf_op jit(solution)/shard_map/reduce_scatter | solution.py:47
  296.1 0.0 copy-done
  296.1 2.2 fusion.14
  298.4 1.2 copy.15
  299.5 211.1 %reduce-scatter.5.cloned.1.call-done = bf16[1,768,1536]{2,1,0:T(8,128)(2,1)} async-done(((bf16[8,768,1536]{2,1,0:T(8,128)(2,1)}), bf16[1,768,1536]{2,1,0:T(8,128)(2,1)}) %reduce-scatter.5.cloned.1.call-update) | async-done | bytes 2359312 | tf_op jit(solution)/shard_map/reduce_scatter | solution.py:37
Async XLA Ops:
  7.2 3.2 copy-start.1
  7.2 210.9 %all-gather.3.cloned.1.call-start = ((), (), s32[]{:S(2)}) async-start(), calls=%async_computation.2 | async-start | bytes 21233664 | tf_op jit(solution)/shard_map/all_gather | solution.py:34
  7.9 247.7 %all-gather.5.cloned.1.call-start = ((), (), s32[]{:S(2)}) async-start(), calls=%async_computation.4 | async-start | bytes 3932160 | tf_op jit(solution)/shard_map/all_gather | solution.py:23
  10.3 285.9 %reduce-scatter.3.cloned.1.call-start = ((), (), s32[]{:S(2)}) async-start(), calls=%async_computation.3 | async-start | bytes 3932160 | tf_op jit(solution)/shard_map/reduce_scatter | solution.py:47
  233.4 277.2 %reduce-scatter.5.cloned.1.call-start = ((), (), s32[]{:S(2)}) async-start(), calls=%async_computation.5 | async-start | bytes 21233664 | tf_op jit(solution)/shard_map/reduce_scatter | solution.py:37
  268.6 27.5 %copy-start = (bf16[256,1536]{0,1:T(8,128)(2,1)S(1)}, bf16[256,1536]{0,1:T(8,128)(2,1)}, u32[]{:S(2)}) copy-start(bf16[256,1536]{0,1:T(8,128)(2,1)} %copy.12) | copy-start | bytes 2359300
Sparse Core Ops, SparseCore 0:
  10.4 207.6 all-gather.2
  220.3 35.2 all-gather.4
  258.0 38.0 reduce-scatter.2
  300.5 210.0 reduce-scatter.4
where the time goes:
time: 517 us
  waiting for transfers between devices  455 us (88%)
  matrix products  19.6 us (4%)
  blocking collectives  13.9 us (3%)
  between operations  13.8 us (3%)
  local copies, waits for them, and re-layouts  8.61 us (2%)
  other arithmetic  5.8 us (1%)
    reduce_scatter x1, waiting for transfers between devices, per_device(): lax.psum_scatter(jnp.einsum('cpr,pd->crd', hidden_split, grad_rows, prefe...  211 us
    all_gather x1, waiting for transfers between devices, per_device(): lax.all_gather(weight, 'gx', axis=1, tiled=True)  194 us
    reduce_scatter x1, waiting for transfers between devices, per_device(): lax.psum_scatter(flat_partial.astype(jnp.bfloat16), 'gz', scatter_dimensi...  27.5 us
    all_gather x1, waiting for transfers between devices, per_device(): full_pre = lax.all_gather(pre_act, 'gz', axis=1, tiled=True)  22.1 us
    all_gather x1, blocking collectives, per_device(): grad_rows = lax.all_gather(grad_out, 'gy', axis=0, tiled=True)  13.9 us
  transfers between devices with their start and end apart: 4, of which 4 were waited for; matrix products, arithmetic and copies ran while one was open for 7% of the time, Pallas kernels for 0%

commit v1 on v0

v1 whole, which is shorter than its diff:
```python
import jax
import jax.numpy as jnp
from jax import lax
from jax.sharding import PartitionSpec as P

tanh_scale = 0.7978845608028654
cubic_coef = 0.044715


def gelu_value(u):
    t = jnp.tanh(tanh_scale * (u + cubic_coef * u * u * u))
    return 0.5 * u * (1.0 + t)


def gelu_slope(u):
    t = jnp.tanh(tanh_scale * (u + cubic_coef * u * u * u))
    return 0.5 * (1.0 + t) + 0.5 * u * (1.0 - t * t) * tanh_scale * (1.0 + 3.0 * cubic_coef * u * u)


def per_device(pre_act, grad_out, weight):
    groups = lax.axis_size("gx")
    tokens, columns = pre_act.shape
    rows = columns // groups
    grad_all = lax.all_gather(grad_out, ("gx", "gy"), axis=0, tiled=True)
    split = pre_act.reshape(tokens, rows, groups).transpose(2, 0, 1)
    mine = lax.all_to_all(split, "gx", split_axis=0, concat_axis=0, tiled=True)
    mine = mine.reshape(groups * tokens, rows)
    own = lax.all_gather(mine, "gz", axis=1, tiled=True)
    hidden = gelu_value(own.astype(jnp.float32)).astype(jnp.bfloat16)
    w = weight.reshape(weight.shape[0], weight.shape[2])
    part = jnp.einsum("td,rd->tr", grad_all, w, preferred_element_type=jnp.float32).astype(jnp.bfloat16)
    summed = lax.psum_scatter(part, "gz", scatter_dimension=1, tiled=True)
    back = lax.all_to_all(
        summed.reshape(groups, tokens, rows), "gx", split_axis=0, concat_axis=0, tiled=True
    )
    back = back.transpose(1, 2, 0).reshape(tokens, columns)
    pre_grad = (back.astype(jnp.float32) * gelu_slope(pre_act.astype(jnp.float32))).astype(jnp.bfloat16)
    weight_grad = jnp.einsum(
        "tr,td->rd", hidden, grad_all, preferred_element_type=jnp.float32
    ).astype(jnp.bfloat16)
    return pre_grad, weight_grad.reshape(weight.shape)


def solution(mesh):
    placed = (P("gx", ("gy", "gz")), P(("gx", "gy"), "gz"), P("gy", "gx", "gz"))
    return jax.shard_map(
        per_device,
        mesh=mesh,
        in_specs=placed,
        out_specs=(P("gx", ("gy", "gz")), P("gy", "gx", "gz")),
        check_vma=False,
    )
```

time: 517 us -> 225 us (0.44)
  waiting for transfers between devices: 455 us -> 155 us
  starting transfers between devices: 0.16 us -> 7.6 us
    reduce_scatter x2 -> x1, waiting for transfers between devices: 239 us -> 21.3 us  [per_device(): summed = lax.psum_scatter(part, 'gz', scatter_dimension=1, tiled=True)]
    all_gather x2, waiting for transfers between devices: 216 us -> 133 us  [the longest x1 98.3 us: per_device(): grad_all = lax.all_gather(grad_out, ('gx', 'gy'), axis=0, tiled=True)]
    all_to_all x0 -> x1, blocking collectives: none -> 18.1 us  [per_device(): mine = lax.all_to_all(split, 'gx', split_axis=0, concat_axis=0, tiled=True)]
    all_gather x1 -> x0, blocking collectives: 13.9 us -> none  [per_device(): grad_rows = lax.all_gather(grad_out, 'gy', axis=0, tiled=True)]
    all_to_all x0 -> x1, starting transfers between devices: none -> 7.48 us  [per_device(): lax.all_to_all(summed.reshape(groups, tokens, rows), 'gx', split_axis=0,...]
  transfers between devices with their start and end apart: 4 -> 4, of which waited for: 4 -> 3; matrix products, arithmetic and copies ran while one was open for 7% -> 7% of each run, Pallas kernels for 0% -> 0%
where the time goes in v1:
time: 225 us; the launch traced here: 224 us
  waiting for transfers between devices  155 us (69%)
  matrix products  19.3 us (9%)
  blocking collectives  18.1 us (8%)
  between operations  13.8 us (6%)
  starting transfers between devices  7.6 us (3%)
  local copies, waits for them, and re-layouts  6.89 us (3%)
  other arithmetic  3.28 us (1%)
    all_gather x1, waiting for transfers between devices, per_device(): grad_all = lax.all_gather(grad_out, ('gx', 'gy'), axis=0, tiled=True)  98.3 us
    all_gather x1, waiting for transfers between devices, per_device(): own = lax.all_gather(mine, 'gz', axis=1, tiled=True)  34.2 us
    reduce_scatter x1, waiting for transfers between devices, per_device(): summed = lax.psum_scatter(part, 'gz', scatter_dimension=1, tiled=True)  21.3 us
    all_to_all x1, blocking collectives, per_device(): mine = lax.all_to_all(split, 'gx', split_axis=0, concat_axis=0, tiled=True)  18.1 us
    dot_general x1, matrix products, per_device(): jnp.einsum('tr,td->rd', hidden, grad_all, preferred_element_type=jnp.floa...  10.1 us
    dot_general x1, matrix products, per_device(): jnp.einsum('td,rd->tr', grad_all, w, preferred_element_type=jnp.float32)  9.23 us
    all_to_all x1, starting transfers between devices, per_device(): lax.all_to_all(summed.reshape(groups, tokens, rows), 'gx', split_axis=0,...  7.48 us
  transfers between devices with their start and end apart: 4, of which 3 were waited for; matrix products, arithmetic and copies ran while one was open for 7% of the time, Pallas kernels for 0%

profile of v1, /device:TPU:0, one launch (start us, length us, event | category | flops | bytes accessed | tf_op | source)
XLA Modules:
  0.0 223.5 jit_solution(667570000639933608)
XLA Ops:
  7.2 0.0 copy-start
  7.2 0.0 all-gather.3.cloned.1.call-start
  7.2 0.7 all-gather.3.cloned.1.call-update
  7.9 0.0 reduce-scatter.2.cloned.1.call-start
  8.0 98.3 %all-gather.3.cloned.1.call-done = bf16[2048,1536]{1,0:T(8,128)(2,1)} async-done(((bf16[64,1536]{1,0:T(8,128)(2,1)}), bf16[2048,1536]{1,0:T(8,128)(2,1)}) %all-gather.3.cloned.1.call-update) | async-done | bytes 6291472 | tf_op jit(solution)/shard_map/all_gather | solution.py:24
  106.3 0.0 copy-done
  106.3 9.2 %convolution_convert_fusion.1 = bf16[2048,768]{0,1:T(8,128)(2,1)} fusion(bf16[2048,1536]{1,0:T(8,128)(2,1)} %all-gather.3.cloned.1.call-done, bf16[768,1,1536]{2,0,1:T(8,128)(2,1)S(1)} %copy-done), kind=kOutput, calls=%fused_computation.18 | convolution fusion | flops 4833411072 | bytes 11796480 | tf_op jit(solution)/shard_map/td,rd->tr/dot_general | solution.py:31
  115.5 0.0 reduce-scatter.2.cloned.1.call-update
  115.5 0.0 all-gather.5.cloned.1.call-start
  115.6 1.4 copy.11
  117.0 0.2 copy.13
  117.2 18.1 %all_to_all.10 = bf16[8,256,192]{1,2,0:T(8,128)(2,1)S(1)} all-to-all(bf16[8,256,192]{1,2,0:T(8,128)(2,1)S(1)} %copy.13), channel_id=1, replica_groups=mesh['gx'=8,'gy'=4,'gz'=4] {'gx'}, dimensions={0} | all-to-all | bytes 1572864 | tf_op jit(solution)/shard_map/all_to_all | solution.py:26
  135.3 1.0 copy.17
  136.3 0.0 all-gather.5.cloned.1.call-update
  136.3 21.3 %reduce-scatter.2.cloned.1.call-done = bf16[2048,192]{0,1:T(8,128)(2,1)} async-done(((bf16[2048,768]{0,1:T(8,128)(2,1)}), bf16[2048,192]{0,1:T(8,128)(2,1)}) %reduce-scatter.2.cloned.1.call-update) | async-done | bytes 786448 | tf_op jit(solution)/shard_map/reduce_scatter | solution.py:32
  157.6 2.1 copy.20
  159.6 7.5 %all-to-all-start = ((bf16[8,256,192]{1,2,0:T(8,128)(2,1)}), bf16[8,256,192]{1,2,0:T(8,128)(2,1)}, u32[]{:S(2)}, u32[]{:S(2)}) async-start(bf16[8,256,192]{1,2,0:T(8,128)(2,1)} %bitcast.22), calls=%async_computation.1 | async-start | bytes 1572864 | tf_op jit(solution)/shard_map/all_to_all | solution.py:33
  167.1 34.2 %all-gather.5.cloned.1.call-done = bf16[2048,768]{0,1:T(8,128)(2,1)} async-done(((bf16[2048,192]{0,1:T(8,128)(2,1)}), bf16[2048,768]{0,1:T(8,128)(2,1)}) %all-gather.5.cloned.1.call-update) | async-done | bytes 3145744 | tf_op jit(solution)/shard_map/all_gather | solution.py:28
  201.3 10.1 %fusion.10 = bf16[768,1,1536]{2,0,1:T(8,128)(2,1)} fusion(bf16[2048,1536]{1,0:T(8,128)(2,1)} %all-gather.3.cloned.1.call-done, bf16[2048,768]{0,1:T(8,128)(2,1)} %all-gather.5.cloned.1.call-done), kind=kOutput, calls=%fused_computation.23 | convolution fusion | flops 4848746496 | bytes 11796480 | tf_op jit(solution)/shard_map/tr,td->rd/dot_general | solution.py:38
  211.4 0.0 all-to-all-done
  211.4 3.3 %fusion.21 = bf16[256,1536]{0,1:T(8,128)(2,1)} fusion(bf16[256,1536]{0,1:T(8,128)(2,1)S(1)} %copy.11, bf16[8,256,192]{1,2,0:T(8,128)(2,1)} %all-to-all-done), kind=kLoop, calls=%fused_computation.32 | loop fusion | flops 8257536 | bytes 2359296 | tf_op jit(solution)/shard_map/convert_element_type | solution.py:37
  214.7 2.3 %copy.15 = bf16[256,1536]{1,0:T(8,128)(2,1)} copy(bf16[256,1536]{0,1:T(8,128)(2,1)} %fusion.21) | data formatting | bytes 1572864
Async XLA Ops:
  7.2 99.1 %copy-start = (bf16[768,1,1536]{2,0,1:T(8,128)(2,1)S(1)}, bf16[768,1,1536]{2,0,1:T(8,128)(2,1)}, u32[]{:S(2)}) copy-start(bf16[768,1,1536]{2,0,1:T(8,128)(2,1)} %param.5) | copy-start | bytes 7077892
  7.2 99.1 %all-gather.3.cloned.1.call-start = ((), (), s32[]{:S(2)}) async-start(), calls=%async_computation.3 | async-start | bytes 6488064 | tf_op jit(solution)/shard_map/all_gather | solution.py:24
  7.9 149.6 %reduce-scatter.2.cloned.1.call-start = ((), (), s32[]{:S(2)}) async-start(), calls=%async_computation.4 | async-start | bytes 3932160 | tf_op jit(solution)/shard_map/reduce_scatter | solution.py:32
  115.5 85.8 %all-gather.5.cloned.1.call-start = ((), (), s32[]{:S(2)}) async-start(), calls=%async_computation.5 | async-start | bytes 3932160 | tf_op jit(solution)/shard_map/all_gather | solution.py:28
  159.6 51.8 %all-to-all-start = ((bf16[8,256,192]{1,2,0:T(8,128)(2,1)}), bf16[8,256,192]{1,2,0:T(8,128)(2,1)}, u32[]{:S(2)}, u32[]{:S(2)}) async-start(bf16[8,256,192]{1,2,0:T(8,128)(2,1)} %bitcast.22), calls=%async_computation.1 | async-start | bytes 1572864 | tf_op jit(solution)/shard_map/all_to_all | solution.py:33
Sparse Core Ops, SparseCore 0:
  11.0 95.2 all-gather.2
  115.7 41.8 reduce-scatter.1
  159.8 41.5 all-gather.4
